TPU v7x, 512 devices: a whole 4x8x8 slice. The times are simulated.
512 devices in a mesh: inst: 16 (over z_lo, x, core), blk: 32 (over y, z_hi).
Axes of the slice: x: 4, y: 8, z: 8 (z_hi: 4, z_lo: 2; z = z_hi * 2 + z_lo), core: 2. Of those that a mesh axis runs over, the one named last changes fastest.
Arguments:
- state: float32 [16, 5, 16, 256, 256], P('inst', None, None, 'blk'), may hold values from -0.53 to 3.9, as said below
- multiples: int32 [7], replicated, may hold values from 1 to 4
Outputs:
- state_change: float32 [16, 5, 16, 256, 256], P('inst', None, None, 'blk')
Inputs may be any that keep to these rules, and one draw needn't show every extreme that they name: `state`: density and pressure lie in 0.7 to 1.3, the axial velocity in 0.2 to 0.8 and the other two velocity components in -0.4 to 0.4; the last variable is the total energy p / 0.4 + rho (u u + v v + w w) / 2.
All inputs are finite; a program needn't handle non-finite values.
Results may differ from a plain program's by a relative error of at most 0.0003.
Values sent between devices are 32-bit elements; how exact they have to be, the bound alone decides.
A program may use at most 64 MiB of HBM per device.

v0:
```python
import math
import jax
import jax.numpy as jnp
from jax import lax
from jax.sharding import PartitionSpec as P

NT = 16
heat_ratio = 1.4
segment_step = 0.05
smooth_weight = 0.5
base_rate = 0.5
diagonal_weight = 3.0


def extended_2(cells, sides, width):
    for axis, dim in sides:
        count = lax.axis_size(axis)
        head = lax.slice_in_dim(cells, 0, width, axis=dim)
        tail = lax.slice_in_dim(cells, cells.shape[dim] - width, cells.shape[dim], axis=dim)
        cells = jnp.concatenate(
            [
                lax.ppermute(tail, axis, [(i, (i + 1) % count) for i in range(count)]),
                cells,
                lax.ppermute(head, axis, [((i + 1) % count, i) for i in range(count)]),
            ],
            axis=dim,
        )
    return cells


def limited(lower, upper):
    return jnp.maximum(0.0, jnp.minimum(lower, upper)) + jnp.minimum(0.0, jnp.maximum(lower, upper))


def take_part(array_in, offset, amount, along):
    return lax.slice_in_dim(array_in, offset, offset + amount, axis=along)


def primitive(conserved):
    density = conserved[:, 0]
    velocity = [conserved[:, 1] / density, conserved[:, 2] / density, conserved[:, 3] / density]
    kinetic = (
        0.5
        * density
        * (velocity[0] * velocity[0] + velocity[1] * velocity[1] + velocity[2] * velocity[2])
    )
    pressure = (heat_ratio - 1.0) * (conserved[:, 4] - kinetic)
    return [density] + velocity + [pressure]


def physical(states, normal):
    density = states[0]
    pressure = states[4]
    velocity = states[1:4]
    normal_speed = velocity[normal]
    energy = pressure / (heat_ratio - 1.0) + 0.5 * density * (
        velocity[0] * velocity[0] + velocity[1] * velocity[1] + velocity[2] * velocity[2]
    )
    conserved = [
        density,
        density * velocity[0],
        density * velocity[1],
        density * velocity[2],
        energy,
    ]
    flux = [density * normal_speed]
    for member in range(3):
        momentum = density * normal_speed * velocity[member]
        if member == normal:
            momentum = momentum + pressure
        flux.append(momentum)
    flux.append((energy + pressure) * normal_speed)
    wave_speed = jnp.abs(normal_speed) + jnp.sqrt(heat_ratio * pressure / density)
    return (flux, conserved, wave_speed)


def divergence(states, along, normal):
    extent = states[0].shape[along]
    interior = extent - 4
    left_side = []
    right_side = []
    for component in states:
        differences = take_part(component, 1, extent - 1, along) - take_part(
            component, 0, extent - 1, along
        )
        slopes = limited(
            take_part(differences, 0, interior + 2, along),
            take_part(differences, 1, interior + 2, along),
        )
        centres = take_part(component, 1, interior + 2, along)
        left_side.append(
            take_part(centres, 0, interior + 1, along)
            + 0.5 * take_part(slopes, 0, interior + 1, along)
        )
        right_side.append(
            take_part(centres, 1, interior + 1, along)
            - 0.5 * take_part(slopes, 1, interior + 1, along)
        )
    left_flux, left_cons, left_speed = physical(left_side, normal)
    right_flux, right_cons, right_speed = physical(right_side, normal)
    wave_speed = jnp.maximum(left_speed, right_speed)
    result = []
    for member in range(5):
        face_flux = 0.5 * (left_flux[member] + right_flux[member]) - 0.5 * wave_speed * (
            right_cons[member] - left_cons[member]
        )
        result.append(
            take_part(face_flux, 1, interior, along) - take_part(face_flux, 0, interior, along)
        )
    return result


def residual(extended):
    states = primitive(extended)
    inner = [component[:, :, 2:-2, :] for component in states]
    circum = divergence(states, 2, 1)
    axial = divergence(
        [jnp.pad(component, ((0, 0), (2, 2), (0, 0), (0, 0)), mode="edge") for component in inner],
        1,
        0,
    )
    radial = divergence(
        [jnp.pad(component, ((0, 0), (0, 0), (0, 0), (2, 2)), mode="edge") for component in inner],
        3,
        2,
    )
    return jnp.stack(
        [axial[member] + circum[member] + radial[member] for member in range(5)], axis=1
    )


def transform_tables(instances):
    indices = jnp.arange(instances, dtype=jnp.int32)
    harmonic = jnp.where(indices < 2, indices * (instances // 2), indices // 2)
    phases = harmonic[:, None] * indices[None, :] % instances
    angles = phases.astype(jnp.float32) * (2.0 * math.pi / instances)
    sine_rows = (indices % 2 == 1) & (indices >= 2)
    basis = jnp.where(sine_rows[:, None], jnp.sin(angles), jnp.cos(angles))
    weights = jnp.where(indices < 2, 1.0 / instances, 2.0 / instances).astype(jnp.float32)
    return (basis * weights[:, None], basis.T)


def pair_solve(right, frequency):
    cosine_part = right[:, 0]
    sine_part = right[:, 1]
    determinant = diagonal_weight * diagonal_weight + frequency * frequency
    return jnp.stack(
        [
            (diagonal_weight * cosine_part - frequency * sine_part) / determinant,
            (diagonal_weight * sine_part + frequency * cosine_part) / determinant,
        ],
        axis=1,
    )


def neighbours(extended):
    circum = extended[:, :, :, :, :-2] + extended[:, :, :, :, 2:]
    middle = extended[:, :, :, :, 1:-1]
    padded = jnp.pad(middle, ((0, 0), (0, 0), (0, 0), (0, 0), (0, 0), (1, 1)))
    return circum + (padded[:, :, :, :, :, :-2] + padded[:, :, :, :, :, 2:])


def body(state, multiples):
    extended = extended_2(state, (("blk", 3),), 4)
    first_sweep = residual(extended)
    segmented = extended[:, :, :, 2:-2] - segment_step * first_sweep
    second_sweep = residual(segmented)
    state_freq, residual_freq = (
        lax.all_to_all(state, "inst", split_axis=2, concat_axis=0, tiled=True),
        lax.all_to_all(second_sweep, "inst", split_axis=2, concat_axis=0, tiled=True),
    )
    forward, inverse = transform_tables(NT)
    layout = residual_freq.shape
    paired = (NT // 2, 2) + layout[1:]
    residual_hat = jnp.dot(
        forward, residual_freq.reshape(NT, -1), precision=lax.Precision.HIGHEST
    ).reshape(paired)
    state_hat = jnp.dot(
        forward, state_freq.reshape(NT, -1), precision=lax.Precision.HIGHEST
    ).reshape(paired)
    frequency = jnp.concatenate(
        [jnp.zeros((1,), jnp.float32), base_rate * multiples.astype(jnp.float32)]
    ).reshape(NT // 2, 1, 1, 1, 1)
    source = jnp.stack([frequency * state_hat[:, 1], -frequency * state_hat[:, 0]], axis=1)
    right_hand = -(residual_hat + source)
    widened = extended_2(right_hand, (("blk", 4),), 3)
    correction = pair_solve(widened, frequency)
    for repeat in range(3):
        trimmed = lax.slice_in_dim(widened, repeat + 1, widened.shape[4] - repeat - 1, axis=4)
        correction = pair_solve(trimmed + smooth_weight * neighbours(correction), frequency)
    change_freq = jnp.dot(
        inverse, correction.reshape(NT, -1), precision=lax.Precision.HIGHEST
    ).reshape(layout)
    return lax.all_to_all(change_freq, "inst", split_axis=0, concat_axis=2, tiled=True)


def solution(mesh):
    return jax.shard_map(
        body,
        mesh=mesh,
        in_specs=(P("inst", None, None, "blk", None), P()),
        out_specs=P("inst", None, None, "blk", None),
        check_vma=False,
    )
```

profile of v0, /device:TPU:25, one launch (start us, length us, event | category | flops | bytes accessed | tf_op | source)
XLA Modules:
  0.0 139.0 jit_solution(2675094903121760378)
XLA Ops:
  0.0 1.5 %fusion.215 = (f32[1,5,16,4,256]{4,3,2,1,0:T(4,128)S(1)}, f32[1,5,16,4,256]{4,3,2,1,0:T(4,128)S(1)}) fusion(f32[1,5,16,8,256]{4,3,2,1,0:T(8,128)} %param.2), kind=kLoop, calls=%fused_computation.532 | loop fusion | bytes 1310720 | tf_op jit(solution)/shard_map/slice | solution.py:19
  1.5 5.8 %collective-permute-start = (f32[1,5,16,4,256]{4,3,2,1,0:T(4,128)S(1)}, f32[1,5,16,4,256]{4,3,2,1,0:T(4,128)S(1)}, u32[]{:S(2)}, u32[]{:S(2)}) collective-permute-start(f32[1,5,16,4,256]{4,3,2,1,0:T(4,128)S(1)} %get-tuple-element.83), channel_id=1, source_target_pairs={{0,1},{1,2},{2,3},{3,4},{4,5},{5,6},{6,7},{7,8},{8,9},{9,10},{10,1... | collective-permute-start | bytes 983048 | tf_op jit(solution)/shard_map/ppermute | solution.py:22
  7.3 6.7 %collective-permute-start.1 = (f32[1,5,16,4,256]{4,3,2,1,0:T(4,128)S(1)}, f32[1,5,16,4,256]{4,3,2,1,0:T(4,128)S(1)}, u32[]{:S(2)}, u32[]{:S(2)}) collective-permute-start(f32[1,5,16,4,256]{4,3,2,1,0:T(4,128)S(1)} %get-tuple-element.84), channel_id=1, source_target_pairs={{1,0},{2,1},{3,2},{4,3},{5,4},{6,5},{7,6},{8,7},{9,8},{10,9},{11,1... | collective-permute-start | bytes 983048 | tf_op jit(solution)/shard_map/ppermute | solution.py:24
  14.0 0.9 copy.86
  14.9 6.2 %all-to-all-start.1 = ((f32[1,5,16,8,256]{4,3,1,0,2:T(8,128)}), f32[1,5,16,8,256]{4,3,1,0,2:T(8,128)S(1)}, u32[]{:S(2)}, u32[]{:S(2)}) async-start(f32[1,5,16,8,256]{4,3,1,0,2:T(8,128)} %copy.86), calls=%async_computation.1 | async-start | bytes 1310720 | tf_op jit(solution)/shard_map/all_to_all | solution.py:169
  21.0 3.3 %collective-permute-done = f32[1,5,16,4,256]{4,3,2,1,0:T(4,128)S(1)} collective-permute-done((f32[1,5,16,4,256]{4,3,2,1,0:T(4,128)S(1)}, f32[1,5,16,4,256]{4,3,2,1,0:T(4,128)S(1)}, u32[]{:S(2)}, u32[]{:S(2)}) %collective-permute-start) | collective-permute-done | bytes 327712 | tf_op jit(solution)/shard_map/ppermute | solution.py:22
  24.3 5.7 %collective-permute-done.1 = f32[1,5,16,4,256]{4,3,2,1,0:T(4,128)S(1)} collective-permute-done((f32[1,5,16,4,256]{4,3,2,1,0:T(4,128)S(1)}, f32[1,5,16,4,256]{4,3,2,1,0:T(4,128)S(1)}, u32[]{:S(2)}, u32[]{:S(2)}) %collective-permute-start.1) | collective-permute-done | bytes 327712 | tf_op jit(solution)/shard_map/ppermute | solution.py:24
  31.4 0.7 multiply_subtract_fusion.5
  37.5 1.4 multiply_subtract_fusion
  38.9 0.8 multiply_subtract_fusion.2
  39.7 0.8 multiply_subtract_fusion.3
  41.1 0.7 multiply_subtract_fusion.1
  42.1 0.9 multiply_subtract_fusion.15
  43.0 0.8 multiply_subtract_fusion.16
  45.6 0.7 fusion.220
  46.8 1.0 multiply_subtract_fusion.25
  47.8 0.9 multiply_subtract_fusion.27
  48.7 0.9 multiply_subtract_fusion.28
  49.6 0.7 slice_subtract_fusion.11
  50.4 0.7 slice_subtract_fusion.12
  51.1 0.7 slice_subtract_fusion.13
  51.9 0.7 slice_subtract_fusion.14
  52.6 0.7 slice_subtract_fusion.15
  54.4 0.6 copy-done.24
  55.2 0.8 minimum_add_fusion.24
  57.1 0.6 copy-done.28
  58.0 0.8 minimum_add_fusion.23
  60.2 0.6 copy-done.20
  61.2 1.6 %copy.101 = f32[1,16,8,1]{2,1,0,3:T(8,128)} copy(f32[1,16,8,1]{3,2,1,0:T(8,128)} %get-tuple-element.103) | data formatting | bytes 1024 | tf_op jit(solution)/shard_map/jit(_pad)/slice | solution.py:123
  62.8 1.6 %copy.102 = f32[1,16,8,1]{2,1,0,3:T(8,128)} copy(f32[1,16,8,1]{3,2,1,0:T(8,128)} %get-tuple-element.104) | data formatting | bytes 1024 | tf_op jit(solution)/shard_map/jit(_pad)/slice | solution.py:123
  64.4 0.8 reshape.866
  65.3 0.8 reshape.867
  66.5 0.8 multiply_subtract_fusion.20
  69.0 0.7 copy-done.2
  69.9 0.9 multiply_subtract_fusion.10
  73.4 0.6 copy-done.16
  74.1 0.9 copy.84
  75.0 7.0 %all-to-all-start = ((f32[1,5,16,8,256]{4,3,1,0,2:T(8,128)}), f32[1,5,16,8,256]{4,3,1,0,2:T(8,128)S(1)}, u32[]{:S(2)}, u32[]{:S(2)}) async-start(f32[1,5,16,8,256]{4,3,1,0,2:T(8,128)} %copy.84), calls=%async_computation | async-start | bytes 1310720 | tf_op jit(solution)/shard_map/all_to_all | solution.py:170
  82.4 0.9 convolution_bitcast_fusion.1
  83.5 9.7 %all-to-all-done = f32[1,5,16,8,256]{4,3,1,0,2:T(8,128)S(1)} async-done(((f32[1,5,16,8,256]{4,3,1,0,2:T(8,128)}), f32[1,5,16,8,256]{4,3,1,0,2:T(8,128)S(1)}, u32[]{:S(2)}, u32[]{:S(2)}) %all-to-all-start) | async-done | bytes 655392 | tf_op jit(solution)/shard_map/all_to_all | solution.py:170
  93.5 0.9 fusion.2
  94.5 4.2 %collective-permute-start.2 = (f32[8,2,5,1,3,256]{5,0,4,2,1,3:T(8,128)S(1)}, f32[8,2,5,1,3,256]{5,0,4,2,1,3:T(8,128)S(1)}, u32[]{:S(2)}, u32[]{:S(2)}) collective-permute-start(f32[8,2,5,1,3,256]{5,0,4,2,1,3:T(8,128)S(1)} %get-tuple-element.81), channel_id=1, source_target_pairs={{0,1},{1,2},{2,3},{3,4},{4,5},{5,6},{6,7},{7,8},{8,9},{9,10},{10,1... | collective-permute-start | bytes 737288 | tf_op jit(solution)/shard_map/ppermute | solution.py:22
  98.7 4.0 %collective-permute-start.3 = (f32[8,2,5,1,3,256]{5,0,4,2,1,3:T(8,128)S(1)}, f32[8,2,5,1,3,256]{5,0,4,2,1,3:T(8,128)S(1)}, u32[]{:S(2)}, u32[]{:S(2)}) collective-permute-start(f32[8,2,5,1,3,256]{5,0,4,2,1,3:T(8,128)S(1)} %get-tuple-element.82), channel_id=1, source_target_pairs={{1,0},{2,1},{3,2},{4,3},{5,4},{6,5},{7,6},{8,7},{9,8},{10,9},{11,1... | collective-permute-start | bytes 737288 | tf_op jit(solution)/shard_map/ppermute | solution.py:24
  102.8 6.5 %collective-permute-done.2 = f32[8,2,5,1,3,256]{5,0,4,2,1,3:T(8,128)S(1)} collective-permute-done((f32[8,2,5,1,3,256]{5,0,4,2,1,3:T(8,128)S(1)}, f32[8,2,5,1,3,256]{5,0,4,2,1,3:T(8,128)S(1)}, u32[]{:S(2)}, u32[]{:S(2)}) %collective-permute-start.2) | collective-permute-done | bytes 245792 | tf_op jit(solution)/shard_map/ppermute | solution.py:22
  109.3 8.0 %collective-permute-done.3 = f32[8,2,5,1,3,256]{5,0,4,2,1,3:T(8,128)S(1)} collective-permute-done((f32[8,2,5,1,3,256]{5,0,4,2,1,3:T(8,128)S(1)}, f32[8,2,5,1,3,256]{5,0,4,2,1,3:T(8,128)S(1)}, u32[]{:S(2)}, u32[]{:S(2)}) %collective-permute-start.3) | collective-permute-done | bytes 245792 | tf_op jit(solution)/shard_map/ppermute | solution.py:24
  120.9 0.8 convolution_bitcast_fusion
  122.1 16.0 %all_to_all.48 = f32[16,5,1,8,256]{4,3,1,2,0:T(8,128)S(1)} all-to-all(f32[16,5,1,8,256]{4,3,1,2,0:T(8,128)S(1)} %copy.91), channel_id=1, replica_groups=mesh['inst'=16,'blk'=32] {'inst'}, dimensions={0} | all-to-all | bytes 1310720 | tf_op jit(solution)/shard_map/all_to_all | solution.py:194
  138.1 0.9 copy.92
  (259 shorter events, 23.2 us)
Async XLA Ops:
  0.0 14.0 %copy-start = (f32[1,5,16,8,256]{4,3,2,1,0:T(8,128)S(1)}, f32[1,5,16,8,256]{4,3,2,1,0:T(8,128)}, u32[]{:S(2)}) copy-start(f32[1,5,16,8,256]{4,3,2,1,0:T(8,128)} %param.2) | copy-start | bytes 1966084
  1.5 22.8 %collective-permute-start = (f32[1,5,16,4,256]{4,3,2,1,0:T(4,128)S(1)}, f32[1,5,16,4,256]{4,3,2,1,0:T(4,128)S(1)}, u32[]{:S(2)}, u32[]{:S(2)}) collective-permute-start(f32[1,5,16,4,256]{4,3,2,1,0:T(4,128)S(1)} %get-tuple-element.83), channel_id=1, source_target_pairs={{0,1},{1,2},{2,3},{3,4},{4,5},{5,6},{6,7},{7,8},{8,9},{9,10},{10,1... | collective-permute-start | bytes 983048 | tf_op jit(solution)/shard_map/ppermute | solution.py:22
  7.3 22.7 %collective-permute-start.1 = (f32[1,5,16,4,256]{4,3,2,1,0:T(4,128)S(1)}, f32[1,5,16,4,256]{4,3,2,1,0:T(4,128)S(1)}, u32[]{:S(2)}, u32[]{:S(2)}) collective-permute-start(f32[1,5,16,4,256]{4,3,2,1,0:T(4,128)S(1)} %get-tuple-element.84), channel_id=1, source_target_pairs={{1,0},{2,1},{3,2},{4,3},{5,4},{6,5},{7,6},{8,7},{9,8},{10,9},{11,1... | collective-permute-start | bytes 983048 | tf_op jit(solution)/shard_map/ppermute | solution.py:24
  14.9 60.2 %all-to-all-start.1 = ((f32[1,5,16,8,256]{4,3,1,0,2:T(8,128)}), f32[1,5,16,8,256]{4,3,1,0,2:T(8,128)S(1)}, u32[]{:S(2)}, u32[]{:S(2)}) async-start(f32[1,5,16,8,256]{4,3,1,0,2:T(8,128)} %copy.86), calls=%async_computation.1 | async-start | bytes 1310720 | tf_op jit(solution)/shard_map/all_to_all | solution.py:169
  46.6 1.2 copy-start.30
  47.8 1.8 %copy-start.6 = (f32[1,17,8,256]{3,2,1,0:T(8,128)}, f32[1,17,8,256]{3,2,1,0:T(8,128)S(1)}, u32[]{:S(2)}) copy-start(f32[1,17,8,256]{3,2,1,0:T(8,128)S(1)} %get-tuple-element.18) | copy-start | bytes 417796
  47.8 1.8 %copy-start.8 = (f32[1,17,8,256]{3,2,1,0:T(8,128)}, f32[1,17,8,256]{3,2,1,0:T(8,128)S(1)}, u32[]{:S(2)}) copy-start(f32[1,17,8,256]{3,2,1,0:T(8,128)S(1)} %get-tuple-element.19) | copy-start | bytes 417796
  47.8 1.8 %copy-start.10 = (f32[1,17,8,256]{3,2,1,0:T(8,128)}, f32[1,17,8,256]{3,2,1,0:T(8,128)S(1)}, u32[]{:S(2)}) copy-start(f32[1,17,8,256]{3,2,1,0:T(8,128)S(1)} %get-tuple-element.20) | copy-start | bytes 417796
  47.8 1.8 %copy-start.12 = (f32[1,17,8,256]{3,2,1,0:T(8,128)}, f32[1,17,8,256]{3,2,1,0:T(8,128)S(1)}, u32[]{:S(2)}) copy-start(f32[1,17,8,256]{3,2,1,0:T(8,128)S(1)} %get-tuple-element.21) | copy-start | bytes 417796
  53.7 0.6 copy-start.22
  54.3 0.6 copy-start.24
  56.4 0.6 copy-start.26
  57.1 0.6 copy-start.28
  60.2 0.6 copy-start.20
  64.4 2.1 %copy-start.14 = (f32[1,16,8,258]{3,2,1,0:T(8,128)S(1)}, f32[1,16,8,258]{3,2,1,0:T(8,128)}, u32[]{:S(2)}) copy-start(f32[1,16,8,258]{3,2,1,0:T(8,128)} %minimum_add_fusion.24) | copy-start | bytes 396292
  64.4 2.1 %copy-start.15 = (f32[1,16,8,258]{3,2,1,0:T(8,128)S(1)}, f32[1,16,8,258]{3,2,1,0:T(8,128)}, u32[]{:S(2)}) copy-start(f32[1,16,8,258]{3,2,1,0:T(8,128)} %minimum_add_fusion.23) | copy-start | bytes 396292
  64.4 2.1 %copy-start.21 = (f32[1,16,8,2]{3,2,1,0:T(8,128)S(1)}, f32[1,16,8,2]{3,2,1,0:T(8,128)}, u32[]{:S(2)}) copy-start(f32[1,16,8,2]{3,2,1,0:T(8,128)} %copy-done.20) | copy-start | bytes 3076
  64.4 2.1 %copy-start.23 = (f32[1,16,8,2]{3,2,1,0:T(8,128)S(1)}, f32[1,16,8,2]{3,2,1,0:T(8,128)}, u32[]{:S(2)}) copy-start(f32[1,16,8,2]{3,2,1,0:T(8,128)} %copy-done.22) | copy-start | bytes 3076
  64.4 2.1 %copy-start.25 = (f32[1,16,8,2]{3,2,1,0:T(8,128)S(1)}, f32[1,16,8,2]{3,2,1,0:T(8,128)}, u32[]{:S(2)}) copy-start(f32[1,16,8,2]{3,2,1,0:T(8,128)} %copy-done.24) | copy-start | bytes 3076
  64.4 2.1 %copy-start.27 = (f32[1,16,8,2]{3,2,1,0:T(8,128)S(1)}, f32[1,16,8,2]{3,2,1,0:T(8,128)}, u32[]{:S(2)}) copy-start(f32[1,16,8,2]{3,2,1,0:T(8,128)} %copy-done.26) | copy-start | bytes 3076
  64.4 2.1 %copy-start.29 = (f32[1,16,8,2]{3,2,1,0:T(8,128)S(1)}, f32[1,16,8,2]{3,2,1,0:T(8,128)}, u32[]{:S(2)}) copy-start(f32[1,16,8,2]{3,2,1,0:T(8,128)} %copy-done.28) | copy-start | bytes 3076
  67.8 1.0 copy-start.5
  67.8 1.0 copy-start.4
  67.8 1.1 copy-start.3
  68.7 1.0 copy-start.2
  68.8 1.0 copy-start.1
  70.8 0.9 copy-start.19
  70.8 1.0 copy-start.18
  71.9 0.9 copy-start.17
  71.9 1.0 copy-start.7
  71.9 1.0 copy-start.9
  71.9 1.1 copy-start.11
  71.9 1.1 copy-start.13
  71.9 1.1 copy-start.31
  73.1 0.9 copy-start.16
  74.1 7.9 %copy-start.32 = (s32[7]{0:T(128)S(1)}, s32[7]{0:T(128)}, u32[]{:S(2)}) copy-start(s32[7]{0:T(128)} %param.3) | copy-start | bytes 88
  75.0 18.2 %all-to-all-start = ((f32[1,5,16,8,256]{4,3,1,0,2:T(8,128)}), f32[1,5,16,8,256]{4,3,1,0,2:T(8,128)S(1)}, u32[]{:S(2)}, u32[]{:S(2)}) async-start(f32[1,5,16,8,256]{4,3,1,0,2:T(8,128)} %copy.84), calls=%async_computation | async-start | bytes 1310720 | tf_op jit(solution)/shard_map/all_to_all | solution.py:170
  94.5 14.8 %collective-permute-start.2 = (f32[8,2,5,1,3,256]{5,0,4,2,1,3:T(8,128)S(1)}, f32[8,2,5,1,3,256]{5,0,4,2,1,3:T(8,128)S(1)}, u32[]{:S(2)}, u32[]{:S(2)}) collective-permute-start(f32[8,2,5,1,3,256]{5,0,4,2,1,3:T(8,128)S(1)} %get-tuple-element.81), channel_id=1, source_target_pairs={{0,1},{1,2},{2,3},{3,4},{4,5},{5,6},{6,7},{7,8},{8,9},{9,10},{10,1... | collective-permute-start | bytes 737288 | tf_op jit(solution)/shard_map/ppermute | solution.py:22
  98.7 18.5 %collective-permute-start.3 = (f32[8,2,5,1,3,256]{5,0,4,2,1,3:T(8,128)S(1)}, f32[8,2,5,1,3,256]{5,0,4,2,1,3:T(8,128)S(1)}, u32[]{:S(2)}, u32[]{:S(2)}) collective-permute-start(f32[8,2,5,1,3,256]{5,0,4,2,1,3:T(8,128)S(1)} %get-tuple-element.82), channel_id=1, source_target_pairs={{1,0},{2,1},{3,2},{4,3},{5,4},{6,5},{7,6},{8,7},{9,8},{10,9},{11,1... | collective-permute-start | bytes 737288 | tf_op jit(solution)/shard_map/ppermute | solution.py:24
where the time goes:
time: 140 us; the launch traced here: 139 us
  starting transfers between devices  33.9 us (24%)
  waiting for transfers between devices  33.1 us (24%)
  other arithmetic  30.4 us (22%)
  local copies, waits for them, and re-layouts  21.4 us (15%)
  blocking collectives  16 us (11%)
  matrix products  2.59 us (2%)
  between operations  1.65 us (1%)
    all_to_all x1, blocking collectives, body(): lax.all_to_all(change_freq, 'inst', split_axis=0, concat_axis=2, tiled=True)  16 us
    sub x20, other arithmetic, divergence(): 0.5 * (left_flux[member] + right_flux[member])  13.7 us
    ppermute x2, waiting for transfers between devices, extended_2(): lax.ppermute(head, axis, [((i + 1) % count, i) for i in range(count)])  13.7 us
    ppermute x2, starting transfers between devices, extended_2(): lax.ppermute(head, axis, [((i + 1) % count, i) for i in range(count)])  10.7 us
    ppermute x2, starting transfers between devices, extended_2(): lax.ppermute(tail, axis, [(i, (i + 1) % count) for i in range(count)])  10.1 us
    ppermute x2, waiting for transfers between devices, extended_2(): lax.ppermute(tail, axis, [(i, (i + 1) % count) for i in range(count)])  9.72 us
    all_to_all x1, waiting for transfers between devices, body(): lax.all_to_all(second_sweep, 'inst', split_axis=2, concat_axis=0, tiled=T...  9.7 us
    unnamed x70, local copies, waits for them, and re-layouts  7.32 us
  transfers between devices with their start and end apart: 6, of which 5 were waited for; matrix products, arithmetic and copies ran while one was open for 29% of the time, Pallas kernels for 0%

commit v1 on v0

--- a/solution.py
+++ b/solution.py
@@ -166,7 +166,12 @@
     segmented = extended[:, :, :, 2:-2] - segment_step * first_sweep
     second_sweep = residual(segmented)
     state_freq, residual_freq = (
-        lax.all_to_all(state, "inst", split_axis=2, concat_axis=0, tiled=True),
+        jnp.concatenate(
+            lax.all_to_all(
+                jnp.stack(jnp.split(state, lax.axis_size("inst"), axis=2)), "inst", 0, 0
+            ),
+            axis=0,
+        ),
         lax.all_to_all(second_sweep, "inst", split_axis=2, concat_axis=0, tiled=True),
     )
     forward, inverse = transform_tables(NT)

time: 140 us -> 139 us (level)
  waiting for transfers between devices: 33.1 us -> 23.8 us
  local copies, waits for them, and re-layouts: 21.4 us -> 30.1 us
    unnamed x70 -> x83, local copies, waits for them, and re-layouts: 7.32 us -> 15.5 us
    ppermute x2, waiting for transfers between devices: 13.7 us -> 7.15 us  [extended_2(): lax.ppermute(head, axis, [((i + 1) % count, i) for i in range(count)])]
    ppermute x2, waiting for transfers between devices: 9.72 us -> 6.65 us  [extended_2(): lax.ppermute(tail, axis, [(i, (i + 1) % count) for i in range(count)])]
  transfers between devices with their start and end apart: 6 -> 6, of which waited for: 5 -> 3; matrix products, arithmetic and copies ran while one was open for 29% -> 35% of each run, Pallas kernels for 0% -> 0%
where the time goes in v1:
time: 139 us
  starting transfers between devices  33.7 us (24%)
  other arithmetic  30.4 us (22%)
  local copies, waits for them, and re-layouts  30.1 us (22%)
  waiting for transfers between devices  23.8 us (17%)
  blocking collectives  16.3 us (12%)
  matrix products  2.59 us (2%)
  between operations  1.66 us (1%)
    all_to_all x1, blocking collectives, body(): lax.all_to_all(change_freq, 'inst', split_axis=0, concat_axis=2, tiled=True)  16.3 us
    unnamed x83, local copies, waits for them, and re-layouts  15.5 us
    sub x20, other arithmetic, divergence(): 0.5 * (left_flux[member] + right_flux[member])  13.7 us
    ppermute x2, starting transfers between devices, extended_2(): lax.ppermute(head, axis, [((i + 1) % count, i) for i in range(count)])  11.4 us
    all_to_all x1, waiting for transfers between devices, body(): lax.all_to_all(second_sweep, 'inst', split_axis=2, concat_axis=0, tiled=T...  10 us
    ppermute x2, starting transfers between devices, extended_2(): lax.ppermute(tail, axis, [(i, (i + 1) % count) for i in range(count)])  9.4 us
    ppermute x2, waiting for transfers between devices, extended_2(): lax.ppermute(head, axis, [((i + 1) % count, i) for i in range(count)])  7.15 us
    all_to_all x1, starting transfers between devices, body(): lax.all_to_all(second_sweep, 'inst', split_axis=2, concat_axis=0, tiled=T...  6.75 us
  transfers between devices with their start and end apart: 6, of which 3 were waited for; matrix products, arithmetic and copies ran while one was open for 35% of the time, Pallas kernels for 0%

profile of v1, /device:TPU:25, one launch (start us, length us, event | category | flops | bytes accessed | tf_op | source)
XLA Modules:
  0.0 138.5 jit_solution(3278713283901938562)
XLA Ops:
  0.0 1.5 %fusion.215 = (f32[1,5,16,4,256]{4,3,2,1,0:T(4,128)S(1)}, f32[1,5,16,4,256]{4,3,2,1,0:T(4,128)S(1)}) fusion(f32[1,5,16,8,256]{4,3,2,1,0:T(8,128)} %param.2), kind=kLoop, calls=%fused_computation.548 | loop fusion | bytes 1310720 | tf_op jit(solution)/shard_map/slice | solution.py:19
  1.5 5.8 %collective-permute-start = (f32[1,5,16,4,256]{4,3,2,1,0:T(4,128)S(1)}, f32[1,5,16,4,256]{4,3,2,1,0:T(4,128)S(1)}, u32[]{:S(2)}, u32[]{:S(2)}) collective-permute-start(f32[1,5,16,4,256]{4,3,2,1,0:T(4,128)S(1)} %get-tuple-element.83), channel_id=1, source_target_pairs={{0,1},{1,2},{2,3},{3,4},{4,5},{5,6},{6,7},{7,8},{8,9},{9,10},{10,1... | collective-permute-start | bytes 983048 | tf_op jit(solution)/shard_map/ppermute | solution.py:22
  7.3 6.7 %collective-permute-start.1 = (f32[1,5,16,4,256]{4,3,2,1,0:T(4,128)S(1)}, f32[1,5,16,4,256]{4,3,2,1,0:T(4,128)S(1)}, u32[]{:S(2)}, u32[]{:S(2)}) collective-permute-start(f32[1,5,16,4,256]{4,3,2,1,0:T(4,128)S(1)} %get-tuple-element.84), channel_id=1, source_target_pairs={{1,0},{2,1},{3,2},{4,3},{5,4},{6,5},{7,6},{8,7},{9,8},{10,9},{11,1... | collective-permute-start | bytes 983048 | tf_op jit(solution)/shard_map/ppermute | solution.py:24
  14.0 0.6 constant_dynamic-update-slice_fusion.15
  14.6 0.6 constant_dynamic-update-slice_fusion.14
  15.2 0.6 constant_dynamic-update-slice_fusion.13
  15.8 0.6 constant_dynamic-update-slice_fusion.12
  23.9 6.2 %all-to-all-start.1 = ((f32[16,1,5,1,8,256]{5,4,2,3,1,0:T(8,128)}), f32[16,1,5,1,8,256]{5,4,2,3,1,0:T(8,128)S(1)}, u32[]{:S(2)}, u32[]{:S(2)}) async-start(f32[16,1,5,1,8,256]{5,4,2,3,1,0:T(8,128)} %constant_dynamic-update-slice_fusion), calls=%async_computation.1 | async-start | bytes 1310720 | tf_op jit(solution)/shard_map/all_to_all | solution.py:170
  31.5 0.7 multiply_subtract_fusion.5
  37.6 1.4 %multiply_subtract_fusion = (f32[1,16,12,257]{3,2,1,0:T(8,128)S(1)}, f32[1,16,12,257]{3,2,1,0:T(8,128)S(1)}, f32[1,16,12,257]{3,2,1,0:T(8,128)S(1)}, f32[1,16,12,257]{3,2,1,0:T(8,128)S(1)}, f32[1,16,12,257]{3,2,1,0:T(8,128)S(1)}) fusion(f32[1,16,12,258]{3,2,1,0:T(8,128)S(1)} %minimum_add_fusion.1, f32[1,16,12,256]{3,2,1,0:T(8,128)S(1)} %slice.1878, ...), kind=kLoop, calls=%fused_computation.105 | loop fusion | flops 3306048 | bytes 3959040 | tf_op jit(solution)/shard_map/sub | solution.py:104
  39.0 0.8 multiply_subtract_fusion.2
  39.8 0.8 multiply_subtract_fusion.3
  41.2 0.7 multiply_subtract_fusion.1
  42.3 0.9 multiply_subtract_fusion.15
  43.2 0.8 multiply_subtract_fusion.16
  45.8 0.7 fusion.220
  47.0 1.0 multiply_subtract_fusion.25
  48.0 0.9 multiply_subtract_fusion.27
  48.8 0.9 multiply_subtract_fusion.28
  49.8 0.7 slice_subtract_fusion.11
  50.5 0.7 slice_subtract_fusion.12
  51.3 0.7 slice_subtract_fusion.13
  52.0 0.7 slice_subtract_fusion.14
  52.7 0.7 slice_subtract_fusion.15
  54.5 0.6 copy-done.24
  55.4 0.8 minimum_add_fusion.24
  57.2 0.6 copy-done.28
  58.1 0.8 minimum_add_fusion.23
  60.3 0.6 copy-done.20
  61.3 1.6 %copy.158 = f32[1,16,8,1]{2,1,0,3:T(8,128)} copy(f32[1,16,8,1]{3,2,1,0:T(8,128)} %get-tuple-element.103) | data formatting | bytes 1024 | tf_op jit(solution)/shard_map/jit(_pad)/slice | solution.py:123
  62.9 1.6 %copy.159 = f32[1,16,8,1]{2,1,0,3:T(8,128)} copy(f32[1,16,8,1]{3,2,1,0:T(8,128)} %get-tuple-element.104) | data formatting | bytes 1024 | tf_op jit(solution)/shard_map/jit(_pad)/slice | solution.py:123
  64.6 0.8 reshape.862
  65.4 0.8 reshape.863
  66.7 0.8 multiply_subtract_fusion.20
  69.1 0.7 copy-done.2
  70.0 0.9 multiply_subtract_fusion.10
  74.2 0.9 copy.127
  75.2 6.7 %all-to-all-start = ((f32[1,5,16,8,256]{4,3,1,0,2:T(8,128)}), f32[1,5,16,8,256]{4,3,1,0,2:T(8,128)S(1)}, u32[]{:S(2)}, u32[]{:S(2)}) async-start(f32[1,5,16,8,256]{4,3,1,0,2:T(8,128)} %copy.127), calls=%async_computation | async-start | bytes 1310720 | tf_op jit(solution)/shard_map/all_to_all | solution.py:175
  82.0 0.9 convolution_bitcast_fusion.1
  83.1 10.0 %all-to-all-done = f32[1,5,16,8,256]{4,3,1,0,2:T(8,128)S(1)} async-done(((f32[1,5,16,8,256]{4,3,1,0,2:T(8,128)}), f32[1,5,16,8,256]{4,3,1,0,2:T(8,128)S(1)}, u32[]{:S(2)}, u32[]{:S(2)}) %all-to-all-start) | async-done | bytes 655392 | tf_op jit(solution)/shard_map/all_to_all | solution.py:175
  93.5 0.9 fusion.2
  94.4 3.6 %collective-permute-start.2 = (f32[8,2,5,1,3,256]{5,0,4,2,1,3:T(8,128)S(1)}, f32[8,2,5,1,3,256]{5,0,4,2,1,3:T(8,128)S(1)}, u32[]{:S(2)}, u32[]{:S(2)}) collective-permute-start(f32[8,2,5,1,3,256]{5,0,4,2,1,3:T(8,128)S(1)} %get-tuple-element.81), channel_id=1, source_target_pairs={{0,1},{1,2},{2,3},{3,4},{4,5},{5,6},{6,7},{7,8},{8,9},{9,10},{10,1... | collective-permute-start | bytes 737288 | tf_op jit(solution)/shard_map/ppermute | solution.py:22
  98.0 4.7 %collective-permute-start.3 = (f32[8,2,5,1,3,256]{5,0,4,2,1,3:T(8,128)S(1)}, f32[8,2,5,1,3,256]{5,0,4,2,1,3:T(8,128)S(1)}, u32[]{:S(2)}, u32[]{:S(2)}) collective-permute-start(f32[8,2,5,1,3,256]{5,0,4,2,1,3:T(8,128)S(1)} %get-tuple-element.82), channel_id=1, source_target_pairs={{1,0},{2,1},{3,2},{4,3},{5,4},{6,5},{7,6},{8,7},{9,8},{10,9},{11,1... | collective-permute-start | bytes 737288 | tf_op jit(solution)/shard_map/ppermute | solution.py:24
  102.7 6.7 %collective-permute-done.2 = f32[8,2,5,1,3,256]{5,0,4,2,1,3:T(8,128)S(1)} collective-permute-done((f32[8,2,5,1,3,256]{5,0,4,2,1,3:T(8,128)S(1)}, f32[8,2,5,1,3,256]{5,0,4,2,1,3:T(8,128)S(1)}, u32[]{:S(2)}, u32[]{:S(2)}) %collective-permute-start.2) | collective-permute-done | bytes 245792 | tf_op jit(solution)/shard_map/ppermute | solution.py:22
  109.4 7.1 %collective-permute-done.3 = f32[8,2,5,1,3,256]{5,0,4,2,1,3:T(8,128)S(1)} collective-permute-done((f32[8,2,5,1,3,256]{5,0,4,2,1,3:T(8,128)S(1)}, f32[8,2,5,1,3,256]{5,0,4,2,1,3:T(8,128)S(1)}, u32[]{:S(2)}, u32[]{:S(2)}) %collective-permute-start.3) | collective-permute-done | bytes 245792 | tf_op jit(solution)/shard_map/ppermute | solution.py:24
  120.2 0.8 convolution_bitcast_fusion
  121.4 16.3 %all_to_all.38 = f32[16,5,1,8,256]{4,3,1,2,0:T(8,128)S(1)} all-to-all(f32[16,5,1,8,256]{4,3,1,2,0:T(8,128)S(1)} %copy.148), channel_id=1, replica_groups=mesh['inst'=16,'blk'=32] {'inst'}, dimensions={0} | all-to-all | bytes 1310720 | tf_op jit(solution)/shard_map/all_to_all | solution.py:199
  137.6 0.9 copy.149
  (272 shorter events, 30.9 us)
Async XLA Ops:
  0.0 14.0 %copy-start = (f32[1,5,16,8,256]{4,3,2,1,0:T(8,128)S(1)}, f32[1,5,16,8,256]{4,3,2,1,0:T(8,128)}, u32[]{:S(2)}) copy-start(f32[1,5,16,8,256]{4,3,2,1,0:T(8,128)} %param.2) | copy-start | bytes 1966084
  1.5 28.6 %collective-permute-start = (f32[1,5,16,4,256]{4,3,2,1,0:T(4,128)S(1)}, f32[1,5,16,4,256]{4,3,2,1,0:T(4,128)S(1)}, u32[]{:S(2)}, u32[]{:S(2)}) collective-permute-start(f32[1,5,16,4,256]{4,3,2,1,0:T(4,128)S(1)} %get-tuple-element.83), channel_id=1, source_target_pairs={{0,1},{1,2},{2,3},{3,4},{4,5},{5,6},{6,7},{7,8},{8,9},{9,10},{10,1... | collective-permute-start | bytes 983048 | tf_op jit(solution)/shard_map/ppermute | solution.py:22
  7.3 22.8 %collective-permute-start.1 = (f32[1,5,16,4,256]{4,3,2,1,0:T(4,128)S(1)}, f32[1,5,16,4,256]{4,3,2,1,0:T(4,128)S(1)}, u32[]{:S(2)}, u32[]{:S(2)}) collective-permute-start(f32[1,5,16,4,256]{4,3,2,1,0:T(4,128)S(1)} %get-tuple-element.84), channel_id=1, source_target_pairs={{1,0},{2,1},{3,2},{4,3},{5,4},{6,5},{7,6},{8,7},{9,8},{10,9},{11,1... | collective-permute-start | bytes 983048 | tf_op jit(solution)/shard_map/ppermute | solution.py:24
  23.9 51.2 %all-to-all-start.1 = ((f32[16,1,5,1,8,256]{5,4,2,3,1,0:T(8,128)}), f32[16,1,5,1,8,256]{5,4,2,3,1,0:T(8,128)S(1)}, u32[]{:S(2)}, u32[]{:S(2)}) async-start(f32[16,1,5,1,8,256]{5,4,2,3,1,0:T(8,128)} %constant_dynamic-update-slice_fusion), calls=%async_computation.1 | async-start | bytes 1310720 | tf_op jit(solution)/shard_map/all_to_all | solution.py:170
  46.8 1.2 copy-start.30
  47.9 1.8 %copy-start.6 = (f32[1,17,8,256]{3,2,1,0:T(8,128)}, f32[1,17,8,256]{3,2,1,0:T(8,128)S(1)}, u32[]{:S(2)}) copy-start(f32[1,17,8,256]{3,2,1,0:T(8,128)S(1)} %get-tuple-element.18) | copy-start | bytes 417796
  47.9 1.8 %copy-start.8 = (f32[1,17,8,256]{3,2,1,0:T(8,128)}, f32[1,17,8,256]{3,2,1,0:T(8,128)S(1)}, u32[]{:S(2)}) copy-start(f32[1,17,8,256]{3,2,1,0:T(8,128)S(1)} %get-tuple-element.19) | copy-start | bytes 417796
  47.9 1.8 %copy-start.10 = (f32[1,17,8,256]{3,2,1,0:T(8,128)}, f32[1,17,8,256]{3,2,1,0:T(8,128)S(1)}, u32[]{:S(2)}) copy-start(f32[1,17,8,256]{3,2,1,0:T(8,128)S(1)} %get-tuple-element.20) | copy-start | bytes 417796
  47.9 1.8 %copy-start.12 = (f32[1,17,8,256]{3,2,1,0:T(8,128)}, f32[1,17,8,256]{3,2,1,0:T(8,128)S(1)}, u32[]{:S(2)}) copy-start(f32[1,17,8,256]{3,2,1,0:T(8,128)S(1)} %get-tuple-element.21) | copy-start | bytes 417796
  53.9 0.6 copy-start.22
  54.5 0.6 copy-start.24
  56.6 0.6 copy-start.26
  57.2 0.6 copy-start.28
  60.3 0.6 copy-start.20
  64.5 2.1 %copy-start.14 = (f32[1,16,8,258]{3,2,1,0:T(8,128)S(1)}, f32[1,16,8,258]{3,2,1,0:T(8,128)}, u32[]{:S(2)}) copy-start(f32[1,16,8,258]{3,2,1,0:T(8,128)} %minimum_add_fusion.24) | copy-start | bytes 396292
  64.5 2.1 %copy-start.15 = (f32[1,16,8,258]{3,2,1,0:T(8,128)S(1)}, f32[1,16,8,258]{3,2,1,0:T(8,128)}, u32[]{:S(2)}) copy-start(f32[1,16,8,258]{3,2,1,0:T(8,128)} %minimum_add_fusion.23) | copy-start | bytes 396292
  64.5 2.1 %copy-start.21 = (f32[1,16,8,2]{3,2,1,0:T(8,128)S(1)}, f32[1,16,8,2]{3,2,1,0:T(8,128)}, u32[]{:S(2)}) copy-start(f32[1,16,8,2]{3,2,1,0:T(8,128)} %copy-done.20) | copy-start | bytes 3076
  64.5 2.1 %copy-start.23 = (f32[1,16,8,2]{3,2,1,0:T(8,128)S(1)}, f32[1,16,8,2]{3,2,1,0:T(8,128)}, u32[]{:S(2)}) copy-start(f32[1,16,8,2]{3,2,1,0:T(8,128)} %copy-done.22) | copy-start | bytes 3076
  64.5 2.1 %copy-start.25 = (f32[1,16,8,2]{3,2,1,0:T(8,128)S(1)}, f32[1,16,8,2]{3,2,1,0:T(8,128)}, u32[]{:S(2)}) copy-start(f32[1,16,8,2]{3,2,1,0:T(8,128)} %copy-done.24) | copy-start | bytes 3076
  64.6 2.1 %copy-start.27 = (f32[1,16,8,2]{3,2,1,0:T(8,128)S(1)}, f32[1,16,8,2]{3,2,1,0:T(8,128)}, u32[]{:S(2)}) copy-start(f32[1,16,8,2]{3,2,1,0:T(8,128)} %copy-done.26) | copy-start | bytes 3076
  64.6 2.1 %copy-start.29 = (f32[1,16,8,2]{3,2,1,0:T(8,128)S(1)}, f32[1,16,8,2]{3,2,1,0:T(8,128)}, u32[]{:S(2)}) copy-start(f32[1,16,8,2]{3,2,1,0:T(8,128)} %copy-done.28) | copy-start | bytes 3076
  67.9 1.0 copy-start.5
  67.9 1.0 copy-start.4
  67.9 1.1 copy-start.3
  68.9 1.0 copy-start.2
  68.9 1.0 copy-start.1
  70.9 0.9 copy-start.19
  70.9 1.0 copy-start.18
  72.0 0.9 copy-start.17
  72.0 1.0 copy-start.7
  72.0 1.0 copy-start.9
  72.1 1.1 copy-start.11
  72.1 1.1 copy-start.13
  72.1 1.1 copy-start.31
  73.2 0.9 copy-start.16
  74.2 7.7 %copy-start.32 = (s32[7]{0:T(128)S(1)}, s32[7]{0:T(128)}, u32[]{:S(2)}) copy-start(s32[7]{0:T(128)} %param.3) | copy-start | bytes 88
  75.2 18.0 %all-to-all-start = ((f32[1,5,16,8,256]{4,3,1,0,2:T(8,128)}), f32[1,5,16,8,256]{4,3,1,0,2:T(8,128)S(1)}, u32[]{:S(2)}, u32[]{:S(2)}) async-start(f32[1,5,16,8,256]{4,3,1,0,2:T(8,128)} %copy.127), calls=%async_computation | async-start | bytes 1310720 | tf_op jit(solution)/shard_map/all_to_all | solution.py:175
  94.4 15.0 %collective-permute-start.2 = (f32[8,2,5,1,3,256]{5,0,4,2,1,3:T(8,128)S(1)}, f32[8,2,5,1,3,256]{5,0,4,2,1,3:T(8,128)S(1)}, u32[]{:S(2)}, u32[]{:S(2)}) collective-permute-start(f32[8,2,5,1,3,256]{5,0,4,2,1,3:T(8,128)S(1)} %get-tuple-element.81), channel_id=1, source_target_pairs={{0,1},{1,2},{2,3},{3,4},{4,5},{5,6},{6,7},{7,8},{8,9},{9,10},{10,1... | collective-permute-start | bytes 737288 | tf_op jit(solution)/shard_map/ppermute | solution.py:22
  98.0 18.5 %collective-permute-start.3 = (f32[8,2,5,1,3,256]{5,0,4,2,1,3:T(8,128)S(1)}, f32[8,2,5,1,3,256]{5,0,4,2,1,3:T(8,128)S(1)}, u32[]{:S(2)}, u32[]{:S(2)}) collective-permute-start(f32[8,2,5,1,3,256]{5,0,4,2,1,3:T(8,128)S(1)} %get-tuple-element.82), channel_id=1, source_target_pairs={{1,0},{2,1},{3,2},{4,3},{5,4},{6,5},{7,6},{8,7},{9,8},{10,9},{11,1... | collective-permute-start | bytes 737288 | tf_op jit(solution)/shard_map/ppermute | solution.py:24
